TPU v7x, 32 devices: a whole 2x2x4 slice. The times are simulated.
32 devices in a mesh: seq: 8 (over z, y), batch: 4 (over x, core).
Axes of the slice: x: 2, y: 2, z: 4, core: 2. Of those that a mesh axis runs over, the one named last changes fastest.
Arguments:
- inputs: bfloat16 [32, 1024, 512], P('batch', 'seq'), may hold values from -6 to 6
- cotangent: bfloat16 [32, 1024, 512], P('batch', 'seq'), may hold values from -6 to 6
- lengths: int32 [32], P('batch'), may hold values from 256 to 1024, as said below
- norm1_gain: float32 [512], replicated, may hold values from 0.25 to 1.75
- norm1_bias: float32 [512], replicated, may hold values from -4 to 4
- qkv_weight: bfloat16 [512, 1536], replicated, may hold values from -0.25 to 0.25
- blend_weights: float32 [3, 8], replicated, may hold values from 0.5 to 4
- out_weight: bfloat16 [512, 512], replicated, may hold values from -1 to 1
- norm2_gain: float32 [512], replicated, may hold values from 0.25 to 1.75
- norm2_bias: float32 [512], replicated, may hold values from -4 to 4
- in_weight: bfloat16 [512, 2048], replicated, may hold values from -0.25 to 0.25
- in_bias: float32 [2048], replicated, may hold values from -4 to 4
- down_weight: bfloat16 [2048, 512], replicated, may hold values from -0.125 to 0.125
- down_bias: float32 [512], replicated, may hold values from -4 to 4
Outputs:
- output: bfloat16 [32, 1024, 512], P('batch', 'seq')
- input_grad: bfloat16 [32, 1024, 512], P('batch', 'seq')
- norm1_gain_grad: float32 [512], replicated
- norm1_bias_grad: float32 [512], replicated
- qkv_weight_grad: float32 [512, 1536], replicated
- blend_grad: float32 [3, 8], replicated
- out_weight_grad: float32 [512, 512], replicated
- norm2_gain_grad: float32 [512], replicated
- norm2_bias_grad: float32 [512], replicated
- in_weight_grad: float32 [512, 2048], replicated
- in_bias_grad: float32 [2048], replicated
- down_weight_grad: float32 [2048, 512], replicated
- down_bias_grad: float32 [512], replicated
Inputs may be any that keep to these rules, and one draw needn't show every extreme that they name: `lengths`: in each aligned group of 8 sequences one, drawn from the seed, has length 1024.
All inputs are finite; a program needn't handle non-finite values.
Results may differ from a plain program's by a relative error of at most 0.009.
Values may be sent and summed in bfloat16 or wider, within the bound.
No kernel may reach another device: no remote copies, remote signals or barrier semaphores. Data moves between devices by JAX's collectives and lax.ppermute only.
A program may use at most 320 MiB of HBM per device.

v0:
```python
import jax
import jax.numpy as jnp
from jax import lax
from jax.sharding import PartitionSpec as P

WINDOW = 30


EPS = 1e-05
NEG = -1e30


def shifted(block, axis, distance):
    devices = range(lax.axis_size(axis))
    route = [(i - distance, i) for i in devices if i - distance in devices]
    return lax.ppermute(block, axis, route)


def entering(value, axis, combine, identity):
    peers, index = (lax.axis_size(axis), lax.axis_index(axis))
    everything = jax.tree.map(
        lambda part, kind: lax.all_gather(part.astype(kind), axis),
        value,
        (jnp.bfloat16, jnp.bfloat16, jnp.bfloat16, jnp.bfloat16),
    )
    start = jax.tree.map(
        lambda part, zero: jnp.broadcast_to(jnp.asarray(zero, part.dtype), part.shape),
        value,
        identity,
    )

    def entering_hop(k, before):
        reached = k < index
        new = combine(
            before, jax.tree.map(lambda part, own: part[k].astype(own.dtype), everything, value)
        )
        return jax.tree.map(lambda a, b: jnp.where(reached, a, b), new, before)

    return lax.fori_loop(0, peers, entering_hop, start)


def carried_in(value, axis, combine, identity):
    peers, index = (lax.axis_size(axis), lax.axis_index(axis))
    everything = jax.tree.map(
        lambda part, kind: lax.all_gather(part.astype(kind), axis),
        value,
        jax.tree.map(lambda a: jnp.bfloat16 if a.dtype == jnp.float32 else a.dtype, value),
    )
    start = jax.tree.map(
        lambda part, zero: jnp.broadcast_to(jnp.asarray(zero, part.dtype), part.shape),
        value,
        identity,
    )

    def carried_hop(k, before):
        at = peers - 1 - k
        reached = at > index
        new = combine(
            before, jax.tree.map(lambda part, own: part[at].astype(own.dtype), everything, value)
        )
        return jax.tree.map(lambda a, b: jnp.where(reached, a, b), new, before)

    return lax.fori_loop(0, peers, carried_hop, start)


def layer_norm(field, gain, shift):
    center = field - jnp.mean(field, axis=-1, keepdims=True)
    spread = jnp.mean(center * center, axis=-1, keepdims=True)
    return center * lax.rsqrt(spread + EPS) * gain + shift


def feature_elu(field):
    return jax.nn.elu(field) + 1.0


def feature_tanh(field):
    return 1.0 + jnp.tanh(field)


def rows_product(left, right):
    return lax.dot_general(
        left, right, (((0,), (0,)), ((), ())), preferred_element_type=jnp.float32
    )


def times_transposed(left, right):
    return lax.dot_general(
        left, right, (((1,), (1,)), ((), ())), preferred_element_type=jnp.float32
    )


def add_states(earlier, later):
    return jax.tree.map(jnp.add, earlier, later)


def local(
    inputs,
    cotangent,
    lengths,
    norm1_gain,
    norm1_bias,
    qkv_weight,
    blend_weights,
    out_weight,
    norm2_gain,
    norm2_bias,
    in_weight,
    in_bias,
    down_weight,
    down_bias,
):
    seq_count, span_len, model_width = inputs.shape
    head_count = blend_weights.shape[1]
    head_size = model_width // head_count
    window = WINDOW
    row_count = seq_count * span_len
    offset = lax.axis_index("seq") * span_len
    bf16 = jnp.bfloat16
    f32 = jnp.float32
    x_float = inputs.reshape(row_count, model_width).astype(f32)
    normed, norm1_back = jax.vjp(layer_norm, x_float, norm1_gain, norm1_bias)
    normed_low = normed.astype(bf16)
    qkv_rows = jnp.dot(normed_low, qkv_weight, preferred_element_type=f32).astype(bf16)
    qkv_rows = qkv_rows.reshape(seq_count, span_len, 3 * model_width)
    four_d = (seq_count, span_len, head_count, head_size)
    queries = qkv_rows[:, :, :model_width].reshape(four_d)
    key_rows = qkv_rows[:, :, model_width : 2 * model_width].reshape(four_d)
    value_rows = qkv_rows[:, :, 2 * model_width :].reshape(four_d)
    kv_tail = qkv_rows[:, span_len - window :, model_width:]
    before = shifted(kv_tail, "seq", 1)
    wide_shape = (seq_count, span_len + window, head_count, head_size)
    key_wide = jnp.concatenate(
        [before[:, :, :model_width], qkv_rows[:, :, model_width : 2 * model_width]], 1
    ).reshape(wide_shape)
    value_wide = jnp.concatenate(
        [before[:, :, model_width:], qkv_rows[:, :, 2 * model_width :]], 1
    ).reshape(wide_shape)
    local_pos = jnp.arange(span_len, dtype=jnp.int32)
    row_pos = (offset + local_pos)[None, :, None]
    col_pos = (offset - window + jnp.arange(span_len + window, dtype=jnp.int32))[None, None, :]
    len_b = lengths[:, None, None]
    allowed = (
        (col_pos >= row_pos - window)
        & (col_pos <= row_pos)
        & (col_pos >= 0)
        & ((col_pos < len_b) | (col_pos == row_pos))
    )
    allowed = allowed[:, None]

    def band_scores():
        return jnp.einsum("srhd,sthd->shrt", queries, key_wide, preferred_element_type=f32) * 0.125

    masked = jnp.where(allowed, band_scores(), NEG)
    row_max = jnp.max(masked, axis=-1, keepdims=True)
    weights = jnp.where(allowed, jnp.exp(masked - row_max), 0.0)
    row_total = jnp.sum(weights, axis=-1, keepdims=True)
    probs = weights / row_total
    log_total = row_max + jnp.log(row_total)
    near_out = jnp.einsum(
        "shrt,sthd->srhd", probs.astype(bf16), value_wide, preferred_element_type=f32
    )
    key_valid = ((offset + local_pos)[None, :] < lengths[:, None]).astype(f32)[:, :, None, None]
    causal = (local_pos[None, :] <= local_pos[:, None]).astype(f32)
    q_float = queries.astype(f32)
    k_float = key_rows.astype(f32)
    kept = []
    contribs = []
    key_sums = []
    for kernel_fn in (feature_elu, feature_tanh):
        fq_val, fq_back = jax.vjp(kernel_fn, q_float)
        fk_val, fk_back = jax.vjp(kernel_fn, k_float)
        fq_low = fq_val.astype(bf16)
        fk_low = (fk_val * key_valid).astype(bf16)
        affinity = (
            jnp.einsum("srhd,sthd->shrt", fq_low, fk_low, preferred_element_type=f32) * causal
        )
        contribs.append(
            jnp.einsum("sthd,sthe->shde", fk_low, value_rows, preferred_element_type=f32)
        )
        key_sums.append(jnp.sum(fk_low.astype(f32), axis=1))
        kept.append((fq_low, fk_low, affinity, fq_back, fk_back))
    state_zero = jnp.zeros((seq_count, head_count, head_size, head_size), f32)
    sum_zero = jnp.zeros((seq_count, head_count, head_size), f32)
    carried = entering(
        (contribs[0], key_sums[0], contribs[1], key_sums[1]),
        "seq",
        add_states,
        (state_zero, sum_zero, state_zero, sum_zero),
    )
    mixture = blend_weights[0][None, None, :, None] * near_out
    far_parts = []
    for branch_id in range(2):
        fq_low, fk_low, affinity, fq_back, fk_back = kept[branch_id]
        state_sum = carried[2 * branch_id]
        norm_sum = carried[2 * branch_id + 1]
        state_low = state_sum.astype(bf16)
        numerator = jnp.einsum(
            "shrt,sthd->srhd", affinity.astype(bf16), value_rows, preferred_element_type=f32
        )
        numerator = numerator + jnp.einsum(
            "srhd,shde->srhe", fq_low, state_low, preferred_element_type=f32
        )
        denominator = jnp.transpose(jnp.sum(affinity, axis=-1), (0, 2, 1)) + jnp.sum(
            fq_low.astype(f32) * norm_sum[:, None], axis=-1
        )
        far_out = numerator / denominator[..., None]
        mixture = mixture + blend_weights[branch_id + 1][None, None, :, None] * far_out
        far_parts.append((state_low, norm_sum, denominator, far_out))
    attended = mixture.reshape(row_count, model_width).astype(bf16)
    first = x_float + jnp.dot(attended, out_weight, preferred_element_type=f32)
    second, norm2_back = jax.vjp(layer_norm, first, norm2_gain, norm2_bias)
    second_low = second.astype(bf16)
    pre_act = jnp.dot(second_low, in_weight, preferred_element_type=f32) + in_bias
    hidden, gelu_back = jax.vjp(jax.nn.gelu, pre_act)
    hidden_low = hidden.astype(bf16)
    result = first + jnp.dot(hidden_low, down_weight, preferred_element_type=f32) + down_bias
    output = result.astype(bf16).reshape(seq_count, span_len, model_width)
    grad_out = cotangent.reshape(row_count, model_width)
    grad_out_f = grad_out.astype(f32)
    grad_down_w = rows_product(hidden_low, grad_out)
    grad_down_b = jnp.sum(grad_out_f, axis=0)
    (grad_pre,) = gelu_back(times_transposed(grad_out, down_weight))
    grad_pre_low = grad_pre.astype(bf16)
    grad_in_b = jnp.sum(grad_pre_low.astype(f32), axis=0)
    grad_in_w = rows_product(second_low, grad_pre_low)
    grad_first_part, grad_gain2, grad_bias2 = norm2_back(times_transposed(grad_pre_low, in_weight))
    grad_first = grad_out_f + grad_first_part
    grad_att_low = grad_first.astype(bf16)
    grad_out_w = rows_product(attended, grad_att_low)
    grad_mix = times_transposed(grad_att_low, out_weight).reshape(four_d)
    blend_rows = [jnp.sum(grad_mix * near_out, axis=(0, 1, 3))]
    grad_near = (blend_weights[0][None, None, :, None] * grad_mix).astype(bf16)
    probs_again = jnp.exp(jnp.where(allowed, band_scores() - log_total, NEG))
    grad_probs = jnp.einsum("srhd,sthd->shrt", grad_near, value_wide, preferred_element_type=f32)
    delta = jnp.sum(probs_again * grad_probs, axis=-1, keepdims=True)
    grad_scores = (probs_again * (grad_probs - delta)).astype(bf16)
    grad_queries = (
        jnp.einsum("shrt,sthd->srhd", grad_scores, key_wide, preferred_element_type=f32) * 0.125
    )
    grad_key_wide = (
        jnp.einsum("shrt,srhd->sthd", grad_scores, queries, preferred_element_type=f32) * 0.125
    )
    grad_value_wide = jnp.einsum(
        "shrt,srhd->sthd", probs_again.astype(bf16), grad_near, preferred_element_type=f32
    )
    grad_keys = grad_key_wide[:, window:]
    grad_values = grad_value_wide[:, window:]
    back_terms = []
    state_grads = []
    sum_grads = []
    for branch_id in range(2):
        fq_low, fk_low, affinity, fq_back, fk_back = kept[branch_id]
        state_low, norm_sum, denominator, far_out = far_parts[branch_id]
        grad_far = blend_weights[branch_id + 1][None, None, :, None] * grad_mix
        blend_rows.append(
            jnp.sum(
                grad_far / blend_weights[branch_id + 1][None, None, :, None] * far_out,
                axis=(0, 1, 3),
            )
        )
        grad_num = (grad_far / denominator[..., None]).astype(bf16)
        grad_den = -jnp.sum(grad_far * far_out, axis=-1) / denominator
        grad_aff = jnp.einsum("srhd,sthd->shrt", grad_num, value_rows, preferred_element_type=f32)
        grad_aff_low = ((grad_aff + jnp.transpose(grad_den, (0, 2, 1))[..., None]) * causal).astype(
            bf16
        )
        grad_fq = jnp.einsum("shrt,sthd->srhd", grad_aff_low, fk_low, preferred_element_type=f32)
        grad_fq = grad_fq + jnp.einsum(
            "srhe,shde->srhd", grad_num, state_low, preferred_element_type=f32
        )
        grad_fq = grad_fq + grad_den[..., None] * norm_sum[:, None]
        state_grads.append(
            jnp.einsum("srhd,srhe->shde", fq_low, grad_num, preferred_element_type=f32)
        )
        sum_grads.append(jnp.sum(fq_low.astype(f32) * grad_den[..., None], axis=1))
        back_terms.append((grad_aff_low, grad_num, grad_fq))
    later = carried_in(
        (state_grads[0], sum_grads[0], state_grads[1], sum_grads[1]),
        "seq",
        add_states,
        (state_zero, sum_zero, state_zero, sum_zero),
    )
    for branch_id in range(2):
        fq_low, fk_low, affinity, fq_back, fk_back = kept[branch_id]
        grad_aff_low, grad_num, grad_fq = back_terms[branch_id]
        later_low = later[2 * branch_id].astype(bf16)
        later_sum = later[2 * branch_id + 1]
        grad_fk = jnp.einsum("shrt,srhd->sthd", grad_aff_low, fq_low, preferred_element_type=f32)
        grad_fk = grad_fk + jnp.einsum(
            "sthe,shde->sthd", value_rows, later_low, preferred_element_type=f32
        )
        grad_fk = (grad_fk + later_sum[:, None]) * key_valid
        grad_values = grad_values + jnp.einsum(
            "shrt,srhd->sthd", affinity.astype(bf16), grad_num, preferred_element_type=f32
        )
        grad_values = grad_values + jnp.einsum(
            "sthd,shde->sthe", fk_low, later_low, preferred_element_type=f32
        )
        (q_part,) = fq_back(grad_fq)
        (k_part,) = fk_back(grad_fk)
        grad_queries = grad_queries + q_part
        grad_keys = grad_keys + k_part
    three_d = (seq_count, window, model_width)
    halo_back = jnp.concatenate(
        [grad_key_wide[:, :window].reshape(three_d), grad_value_wide[:, :window].reshape(three_d)],
        -1,
    )
    received = shifted(halo_back.astype(jnp.bfloat16), "seq", -1).astype(halo_back.dtype)
    grad_kv = jnp.concatenate(
        [
            grad_keys.reshape(seq_count, span_len, model_width),
            grad_values.reshape(seq_count, span_len, model_width),
        ],
        -1,
    )
    grad_kv = grad_kv + jnp.pad(received, ((0, 0), (span_len - window, 0), (0, 0)))
    grad_qkv = jnp.concatenate(
        [grad_queries.reshape(seq_count, span_len, model_width), grad_kv], -1
    )
    grad_qkv = grad_qkv.reshape(row_count, 3 * model_width).astype(bf16)
    grad_qkv_w = rows_product(normed_low, grad_qkv)
    grad_x_part, grad_gain1, grad_bias1 = norm1_back(times_transposed(grad_qkv, qkv_weight))
    input_grad = (grad_first + grad_x_part).astype(bf16).reshape(seq_count, span_len, model_width)
    grad_blend = jnp.stack(blend_rows, 0)
    summed = lax.psum(
        (
            grad_gain1,
            grad_bias1,
            grad_qkv_w,
            grad_blend,
            grad_out_w,
            grad_gain2,
            grad_bias2,
            grad_in_w,
            grad_in_b,
            grad_down_w,
            grad_down_b,
        ),
        ("seq", "batch"),
    )
    return (output, input_grad) + tuple(summed)


def solution(mesh):
    in_specs = (
        P("batch", "seq", None),
        P("batch", "seq", None),
        P("batch"),
        P(),
        P(),
        P(),
        P(),
        P(),
        P(),
        P(),
        P(),
        P(),
        P(),
        P(),
    )
    out_specs = (
        P("batch", "seq", None),
        P("batch", "seq", None),
        P(),
        P(),
        P(),
        P(),
        P(),
        P(),
        P(),
        P(),
        P(),
        P(),
        P(),
    )
    return jax.shard_map(local, mesh=mesh, in_specs=in_specs, out_specs=out_specs, check_vma=False)
```

profile of v0, /device:TPU:0, one launch (start us, length us, event | category | flops | bytes accessed | tf_op | source)
XLA Modules:
  0.0 988.2 jit_solution(359170895787068393)
XLA Ops:
  34.0 5.7 collective-permute-start
  52.5 46.1 %all_gather.47 = bf16[8,8,8,64]{3,2,1,0:T(8,128)(2,1)} all-gather(bf16[1,8,8,64]{3,2,1,0:T(8,128)(2,1)S(1)} %all_gather.46), channel_id=1, replica_groups=mesh['seq'=8,'batch'=4] {'seq'}, dimensions={0}, use_global_device_ids=true | all-gather | bytes 73728 | tf_op jit(solution)/shard_map/all_gather | solution.py:22
  98.6 33.6 %all_gather.51 = bf16[8,8,8,64]{3,2,1,0:T(8,128)(2,1)} all-gather(bf16[1,8,8,64]{3,2,1,0:T(8,128)(2,1)S(1)} %all_gather.50), channel_id=1, replica_groups=mesh['seq'=8,'batch'=4] {'seq'}, dimensions={0}, use_global_device_ids=true | all-gather | bytes 73728 | tf_op jit(solution)/shard_map/all_gather | solution.py:22
  157.6 11.2 %all-gather.9.cloned.1.call-done = bf16[64,8,64,64]{3,2,1,0:T(8,128)(2,1)} async-done(((bf16[8,8,64,64]{3,2,1,0:T(8,128)(2,1)}), bf16[64,8,64,64]{3,2,1,0:T(8,128)(2,1)}) %all-gather.9.cloned.1.call-update) | async-done | bytes 4194320 | tf_op jit(solution)/shard_map/all_gather | solution.py:22
  168.8 125.3 %all-gather.11.cloned.1.call-done = bf16[64,8,64,64]{3,2,1,0:T(8,128)(2,1)} async-done(((bf16[8,8,64,64]{3,2,1,0:T(8,128)(2,1)}), bf16[64,8,64,64]{3,2,1,0:T(8,128)(2,1)}) %all-gather.11.cloned.1.call-update) | async-done | bytes 4194320 | tf_op jit(solution)/shard_map/all_gather | solution.py:22
  294.1 52.4 %while.42 = (s32[]{:T(128)}, f32[8,8,64,64]{3,2,1,0:T(8,128)}, f32[8,8,64]{2,1,0:T(8,128)S(1)}, f32[8,8,64,64]{3,2,1,0:T(8,128)}, f32[8,8,64]{2,1,0:T(8,128)S(1)...) while((s32[]{:T(128)}, f32[8,8,64,64]{3,2,1,0:T(8,128)}, ...), condition=%wide.region_7.8_spmd.clone, body=%wide.region_6.7_spmd.clone.sunk | while | flops 2129924 | bytes 5324947 | solution.py:39
  299.5 5.9 add_select_fusion.12
  306.2 5.9 add_select_fusion.12
  312.9 5.9 add_select_fusion.12
  319.7 5.9 add_select_fusion.12
  326.4 5.9 add_select_fusion.12
  333.1 5.9 add_select_fusion.12
  339.8 5.9 add_select_fusion.12
  360.3 16.3 %multiply_convert_fusion = (bf16[1024,2048]{1,0:T(8,128)(2,1)}, f32[1024,2048]{1,0:T(8,128)S(1)}) fusion(f32[2048]{0:T(1024)S(1)} %copy-done.115, bf16[512,2048]{1,0:T(8,128)(2,1)S(1)} %copy-done, f32[1024,512]{1,0:T(8,128)S(1)} %get-tuple-element.611, f32[512]{0:T(512)S(1)} %copy-done.96, f32[512]{0:T(512)S(1)} %copy-done.93, f32[1024]{0:T(1024)S(1)} %fusion.108, ...), kind=kOutput, calls=%fused_computation.18 | convolution fusion | flops 2171076608 | bytes 16797696 | tf_op jit(solution)/shard_map/dot_general | solution.py:213
  376.7 8.6 convert_reduce_fusion
  420.2 6.5 multiply_reduce_fusion
  478.9 46.3 %all_gather.54 = bf16[8,8,8,64]{3,2,1,0:T(8,128)(2,1)S(1)} all-gather(bf16[1,8,8,64]{3,2,1,0:T(8,128)(2,1)S(1)} %convert_element_type.352), channel_id=1, replica_groups=mesh['seq'=8,'batch'=4] {'seq'}, dimensions={0}, use_global_device_ids=true | all-gather | bytes 73728 | tf_op jit(solution)/shard_map/all_gather | solution.py:45
  525.2 33.6 %all_gather.57 = bf16[8,8,8,64]{3,2,1,0:T(8,128)(2,1)} all-gather(bf16[1,8,8,64]{3,2,1,0:T(8,128)(2,1)S(1)} %convert_element_type.357), channel_id=1, replica_groups=mesh['seq'=8,'batch'=4] {'seq'}, dimensions={0}, use_global_device_ids=true | all-gather | bytes 73728 | tf_op jit(solution)/shard_map/all_gather | solution.py:45
  582.7 78.7 %all-gather.13.cloned.1.call-done = bf16[64,8,64,64]{3,2,1,0:T(8,128)(2,1)} async-done(((bf16[8,8,64,64]{3,2,1,0:T(8,128)(2,1)}), bf16[64,8,64,64]{3,2,1,0:T(8,128)(2,1)}) %all-gather.13.cloned.1.call-update) | async-done | bytes 4194320 | tf_op jit(solution)/shard_map/all_gather | solution.py:45
  661.3 47.5 %while.43 = (s32[]{:T(128)}, f32[8,8,64,64]{3,2,1,0:T(8,128)S(1)}, f32[8,8,64]{2,1,0:T(8,128)S(1)}, f32[8,8,64,64]{3,2,1,0:T(8,128)}, f32[8,8,64]{2,1,0:T(8,128)...) while((s32[]{:T(128)}, f32[8,8,64,64]{3,2,1,0:T(8,128)S(1)}, ...), condition=%wide.region_22.23_spmd.clone, body=%wide.region_21.22_spmd.clone.sunk | while | flops 2129928 | bytes 5325009 | solution.py:63
  666.9 5.2 add_select_fusion.14
  672.9 5.2 add_select_fusion.14
  678.9 5.2 add_select_fusion.14
  684.9 5.2 add_select_fusion.14
  690.9 5.2 add_select_fusion.14
  696.9 5.2 add_select_fusion.14
  702.9 5.2 add_select_fusion.14
  713.6 5.1 fusion.48
  721.8 6.3 fusion.47
  740.3 7.2 add_convert_fusion.1
  752.1 39.7 %all-reduce.1 = (f32[512]{0:T(512)}, f32[512]{0:T(512)}, f32[3,8]{1,0:T(4,128)}, f32[512]{0:T(512)}, f32[512]{0:T(512)}, /*index=5*/f32[2048]{0:T(1024)}, f32[512]{0:T(512)}) all-reduce(f32[512]{0:T(512)S(1)} %get-tuple-element.510, f32[512]{0:T(512)S(1)} %get-tuple-element.521, ...), channel_id=1, replica_groups=mesh['seq'=8,'batch'=4] {'seq','batch'}, use_global_device_ids=true, to_apply=%region_26.27 | all-reduce | flops 4632 | bytes 37056 | tf_op jit(solution)/shard_map/psum | solution.py:325
  795.1 174.6 %all-reduce.5.cloned.1.call-done = (f32[512,1536]{1,0:T(8,128)}, f32[512,512]{1,0:T(8,128)}, f32[512,2048]{1,0:T(8,128)}, f32[2048,512]{1,0:T(8,128)}) async-done(((f32[512,1536]{1,0:T(8,128)}, f32[512,512]{1,0:T(8,128)}, f32[512,2048]{1,0:T(8,128)}, f32[2048,512]{1,0:T(8,128)}), (f32[512,1536]{1,0:T(8,128)}, f32[512,512]{1,0:T(8,128)}, f32[512,2048]{1,0:T(8,128)}, ...) | async-done | bytes 12582928 | tf_op jit(solution)/shard_map/psum | solution.py:325
  (396 shorter events, 249.5 us)
Async XLA Ops:
  7.2 352.8 %copy-start = (bf16[512,2048]{1,0:T(8,128)(2,1)S(1)}, bf16[512,2048]{1,0:T(8,128)(2,1)}, u32[]{:S(2)}) copy-start(bf16[512,2048]{1,0:T(8,128)(2,1)} %param.28) | copy-start | bytes 6291460
  7.2 161.6 %all-gather.9.cloned.1.call-start = ((), (), s32[]{:S(2)}) async-start(), calls=%async_computation | async-start | bytes 9437184 | tf_op jit(solution)/shard_map/all_gather | solution.py:22
  29.0 265.1 %all-gather.11.cloned.1.call-start = ((), (), s32[]{:S(2)}) async-start(), calls=%async_computation.1 | async-start | bytes 9437184 | tf_op jit(solution)/shard_map/all_gather | solution.py:22
  32.0 550.7 %all-gather.15.cloned.1.call-start = ((), (), s32[]{:S(2)}) async-start(), calls=%async_computation.3 | async-start | bytes 9437184 | tf_op jit(solution)/shard_map/all_gather | solution.py:45
  34.0 102.5 %collective-permute-start = (bf16[8,30,1024]{2,1,0:T(8,128)(2,1)}, bf16[8,30,1024]{2,1,0:T(8,128)(2,1)}, u32[]{:S(2)}, u32[]{:S(2)}) collective-permute-start(bf16[8,30,1024]{2,1,0:T(8,128)(2,1)} %slice.61), channel_id=1, source_target_pairs={{0,4},{4,8},{8,12},{12,16},{16,20},{20,24},{24,28},{1,5},{5,9},{9,... | collective-permute-start | bytes 1474568 | tf_op jit(solution)/shard_map/ppermute | solution.py:16
  51.8 297.6 %copy-start.76 = (f32[8,8,128]{2,1,0:T(8,128)}, f32[8,8,128]{2,1,0:T(8,128)S(1)}, u32[]{:S(2)}) copy-start(f32[8,8,128]{2,1,0:T(8,128)S(1)} %get-tuple-element.525) | copy-start | bytes 98308
  51.8 297.6 %copy-start.75 = (f32[8,8,128]{2,1,0:T(8,128)}, f32[8,8,128]{2,1,0:T(8,128)S(1)}, u32[]{:S(2)}) copy-start(f32[8,8,128]{2,1,0:T(8,128)S(1)} %get-tuple-element.526) | copy-start | bytes 98308
  52.3 301.9 %copy-start.99 = (f32[8]{0:T(128)}, f32[8]{0:T(128)S(1)}, u32[]{:S(2)}) copy-start(f32[8]{0:T(128)S(1)} %get-tuple-element.600) | copy-start | bytes 100
  52.3 301.9 %copy-start.104 = (f32[8]{0:T(128)}, f32[8]{0:T(128)S(1)}, u32[]{:S(2)}) copy-start(f32[8]{0:T(128)S(1)} %get-tuple-element.601) | copy-start | bytes 100
  153.1 201.1 %copy-start.72 = (f32[8,8,128]{2,1,0:T(8,128)}, f32[8,8,128]{2,1,0:T(8,128)S(1)}, u32[]{:S(2)}) copy-start(f32[8,8,128]{2,1,0:T(8,128)S(1)} %get-tuple-element.605) | copy-start | bytes 98308
  346.5 7.7 slice-start
  349.4 42.7 %copy-start.74 = (f32[8,128,8]{1,2,0:T(8,128)}, f32[8,128,8]{1,2,0:T(8,128)S(1)}, u32[]{:S(2)}) copy-start(f32[8,128,8]{1,2,0:T(8,128)S(1)} %bitcast_add_fusion.6) | copy-start | bytes 98308
  350.0 42.1 %copy-start.73 = (f32[8,128,8]{1,2,0:T(8,128)}, f32[8,128,8]{1,2,0:T(8,128)S(1)}, u32[]{:S(2)}) copy-start(f32[8,128,8]{1,2,0:T(8,128)S(1)} %bitcast_add_fusion.5) | copy-start | bytes 98308
  359.5 29.1 %copy-start.17 = (f32[1024,512]{1,0:T(8,128)}, f32[1024,512]{1,0:T(8,128)S(1)}, u32[]{:S(2)}) copy-start(f32[1024,512]{1,0:T(8,128)S(1)} %get-tuple-element.611) | copy-start | bytes 6291460
  360.3 16.3 %copy-start.46 = (bf16[8,128,512]{2,1,0:T(8,128)(2,1)S(1)}, bf16[8,128,512]{2,1,0:T(8,128)(2,1)}, u32[]{:S(2)}) copy-start(bf16[8,128,512]{2,1,0:T(8,128)(2,1)} %param.19) | copy-start | bytes 3145732
  360.3 16.3 %copy-start.112 = (bf16[2048,512]{1,0:T(8,128)(2,1)S(1)}, bf16[2048,512]{1,0:T(8,128)(2,1)}, u32[]{:S(2)}) copy-start(bf16[2048,512]{1,0:T(8,128)(2,1)} %param.30) | copy-start | bytes 6291460
  398.9 262.5 %all-gather.13.cloned.1.call-start = ((), (), s32[]{:S(2)}) async-start(), calls=%async_computation.2 | async-start | bytes 9437184 | tf_op jit(solution)/shard_map/all_gather | solution.py:45
  418.7 551.0 %all-reduce.5.cloned.1.call-start = ((), (), s32[]{:S(2)}) async-start(), calls=%async_computation.4 | async-start | bytes 25165824 | tf_op jit(solution)/shard_map/psum | solution.py:325
  419.2 7.4 slice-start.2
  420.1 9.3 copy-start.80
  420.2 6.5 slice-start.3
  459.0 6.9 copy-start.79
  464.5 266.7 %collective-permute-start.1 = (bf16[8,30,1024]{2,1,0:T(8,128)(2,1)}, bf16[8,30,1024]{2,1,0:T(8,128)(2,1)}, u32[]{:S(2)}, u32[]{:S(2)}) collective-permute-start(bf16[8,30,1024]{2,1,0:T(8,128)(2,1)} %pad_maximum_fusion.5), channel_id=1, source_target_pairs={{4,0},{8,4},{12,8},{16,12},{20,16},{24,20},{28,24},{5,1},{9,5},{13... | collective-permute-start | bytes 1474568 | tf_op jit(solution)/shard_map/ppermute | solution.py:16
  478.9 83.1 %copy-start.14 = (bf16[8,128,512]{1,2,0:T(8,128)(2,1)S(1)}, bf16[8,128,512]{1,2,0:T(8,128)(2,1)}, u32[]{:S(2)}) copy-start(bf16[8,128,512]{1,2,0:T(8,128)(2,1)} %copy.82) | copy-start | bytes 3145732
  478.9 83.1 %copy-start.50 = (bf16[8,8,128,128]{2,3,1,0:T(8,128)(2,1)S(1)}, bf16[8,8,128,128]{2,3,1,0:T(8,128)(2,1)}, u32[]{:S(2)}) copy-start(bf16[8,8,128,128]{2,3,1,0:T(8,128)(2,1)} %copy-done.49) | copy-start | bytes 6291460
  740.3 7.2 copy-start.27
  740.3 7.2 copy-start.61
  740.3 7.2 copy-start.66
  740.3 7.2 copy-start.86
  740.3 7.2 copy-start.95
  740.3 7.2 copy-start.114
  749.6 42.1 %copy-start.33 = (f32[1024,512]{1,0:T(8,128)S(1)}, f32[1024,512]{1,0:T(8,128)}, u32[]{:S(2)}) copy-start(f32[1024,512]{1,0:T(8,128)} %copy-done.32) | copy-start | bytes 6291460
  (97 other events, 262.7 us)
Sparse Core Ops, SparseCore 0:
  29.1 139.6 all-gather.8
  170.9 123.1 all-gather.10
  399.0 136.4 all-gather.14
  538.0 123.2 all-gather.12
  738.5 231.1 all-reduce.4
where the time goes:
time: 994 us; the launch traced here: 988 us
  waiting for transfers between devices  390 us (39%)
  blocking collectives  199 us (20%)
  other arithmetic  146 us (15%)
  matrix products  143 us (14%)
  local copies, waits for them, and re-layouts  85.7 us (9%)
  between operations  15.3 us (2%)
    psum x1, waiting for transfers between devices, local(): lax.psum((grad_gain1, grad_bias1, grad_qkv_w, grad_blend, grad_out_w, gra...  175 us
    all_gather x2, waiting for transfers between devices, entering(): lax.all_gather(part.astype(kind), axis)  136 us
    all_gather x2, blocking collectives, carried_in(): lax.all_gather(part.astype(kind), axis)  79.9 us
    all_gather x2, blocking collectives, entering(): lax.all_gather(part.astype(kind), axis)  79.7 us
    all_gather x2, waiting for transfers between devices, carried_in(): lax.all_gather(part.astype(kind), axis)  78.7 us
    select_n x16, other arithmetic, entering_hop(): return jax.tree.map(lambda a, b: jnp.where(reached, a, b), new, before)  52.2 us
    select_n x16, other arithmetic, carried_hop(): return jax.tree.map(lambda a, b: jnp.where(reached, a, b), new, before)  47 us
    psum x1, blocking collectives, local(): lax.psum((grad_gain1, grad_bias1, grad_qkv_w, grad_blend, grad_out_w, gra...  39.7 us
  transfers between devices with their start and end apart: 7, of which 4 were waited for; matrix products, arithmetic and copies ran while one was open for 22% of the time, Pallas kernels for 0%

commit v1 on v0

v1 whole, which is shorter than its diff:
```python
import functools

import jax
import jax.numpy as jnp
from jax import lax
from jax.experimental import pallas as pl
from jax.experimental.pallas import tpu as pltpu
from jax.sharding import PartitionSpec as P

WINDOW = 30
HEAD = 64
PAIR = 2 * HEAD
TILE = 64
EPS = 1e-05
NEG = -1e30
BF16 = jnp.bfloat16
F32 = jnp.float32


def layer_norm(field, gain, shift):
    center = field - jnp.mean(field, axis=-1, keepdims=True)
    spread = jnp.mean(center * center, axis=-1, keepdims=True)
    return center * lax.rsqrt(spread + EPS) * gain + shift


def rows_product(left, right):
    return lax.dot_general(
        left, right, (((0,), (0,)), ((), ())), preferred_element_type=F32
    )


def times_transposed(left, right):
    return lax.dot_general(
        left, right, (((1,), (1,)), ((), ())), preferred_element_type=F32
    )


def times(left, right):
    return lax.dot_general(
        left, right, (((1,), (0,)), ((), ())), preferred_element_type=F32
    )


def split_heads(block):
    lane = lax.broadcasted_iota(jnp.int32, block.shape, 1)
    zero = jnp.zeros_like(block)
    return jnp.concatenate(
        [jnp.where(lane < HEAD, block, zero), jnp.where(lane < HEAD, zero, block)], 0
    )


def same_head(rows, lanes):
    row = lax.broadcasted_iota(jnp.int32, (rows, lanes), 0) % PAIR
    lane = lax.broadcasted_iota(jnp.int32, (rows, lanes), 1) % PAIR
    return (row // HEAD) == (lane // HEAD)


def elu_feature(field):
    return jnp.where(field > 0, field + 1.0, jnp.exp(jnp.minimum(field, 0.0)))


def tanh_feature(field):
    return 1.0 + jnp.tanh(field)


def fill_features(meta_ref, qkv_ref, halo_ref, kpad, vpad, fq, fk, rows, width):
    chunk = 2 * TILE
    zero = jnp.zeros((TILE, width), BF16)
    kpad[:TILE, :] = halo_ref[:, :width] * 0.125
    vpad[:TILE, :] = halo_ref[:, width:]
    for c in range(2):
        fk[c, :TILE, :] = zero
    length, offset = meta_ref[0], meta_ref[1]

    def fill(step, carry):
        at = pl.multiple_of(step * chunk, chunk)
        here, there = pl.ds(at, chunk), pl.ds(at + TILE, chunk)
        q = qkv_ref[here, :width].astype(F32)
        k_low = qkv_ref[here, width : 2 * width]
        k = k_low.astype(F32)
        position = offset + at + lax.broadcasted_iota(jnp.int32, (chunk, width), 0)
        valid = position < length
        kpad[there, :] = k_low * 0.125
        vpad[there, :] = qkv_ref[here, 2 * width :]
        for c, feature in enumerate((elu_feature, tanh_feature)):
            fq[c, here, :] = feature(q).astype(BF16)
            fk[c, there, :] = jnp.where(valid, feature(k), 0.0).astype(BF16)
        return carry

    lax.fori_loop(0, rows // chunk, fill, 0)


def tile_masks(meta_ref, tile):
    shape = (TILE, 2 * PAIR)
    row = lax.broadcasted_iota(jnp.int32, shape, 0)
    lane = lax.broadcasted_iota(jnp.int32, shape, 1) % PAIR
    back = row + TILE - lane
    key = meta_ref[1] + (tile - 1) * TILE + lane
    known = (key >= 0) & (key < meta_ref[0])
    near = (back >= 0) & (back <= WINDOW) & (known | (back == 0))
    return near, back >= 0


def tile_scores(q, keys, fq, fks, near_mask, far_mask):
    scores = jnp.where(near_mask, times_transposed(q, keys), NEG)
    halves = []
    for h in range(2):
        part = scores[:, h * PAIR : (h + 1) * PAIR]
        part = jnp.exp(part - jnp.max(part, axis=1, keepdims=True))
        halves.append(part / jnp.sum(part, axis=1, keepdims=True))
    probs = jnp.concatenate(halves, 1)
    far = [jnp.where(far_mask, times_transposed(fq[c], fks[c]), 0.0) for c in range(2)]
    return probs, far[0], far[1]


def attend_kernel(
    rows, width, meta_ref, blend_ref, qkv_ref, halo_ref, state_ref, att_ref, total_ref,
    kpad, vpad, fq, fk, state,
):
    pairs = width // PAIR
    fill_features(meta_ref, qkv_ref, halo_ref, kpad, vpad, fq, fk, rows, width)
    state[...] = state_ref[...]
    ones = same_head(2 * PAIR, PAIR)
    ones = jnp.where(
        (lax.broadcasted_iota(jnp.int32, (2 * PAIR, PAIR), 0) // PAIR)
        == (lax.broadcasted_iota(jnp.int32, (2 * PAIR, PAIR), 1) // HEAD),
        1.0,
        0.0,
    ).astype(BF16)
    block = same_head(PAIR, 2 * PAIR)
    plain_ones = jnp.ones((TILE, PAIR), BF16)

    def step(tile, carry):
        at = pl.multiple_of(tile * TILE, TILE)
        here, window = pl.ds(at, TILE), pl.ds(at, 2 * TILE)
        near_mask, far_mask = tile_masks(meta_ref, tile)
        for p in range(pairs):
            lanes = slice(p * PAIR, (p + 1) * PAIR)
            q = qkv_ref[here, lanes]
            keys = split_heads(kpad[window, lanes])
            values = vpad[window, lanes]
            wide = jnp.concatenate([split_heads(values), ones], 1)
            feats = [fq[c, here, lanes] for c in range(2)]
            fkw = [fk[c, window, lanes] for c in range(2)]
            probs, far1, far2 = tile_scores(
                q, keys, feats, [split_heads(f) for f in fkw], near_mask, far_mask
            )
            stack = jnp.concatenate([probs, far1, far2], 0).astype(BF16)
            sums = times(stack, wide)
            mixed = blend_ref[0:1, lanes] * sums[:TILE, :PAIR]
            for c in range(2):
                mine = sums[(c + 1) * TILE : (c + 2) * TILE]
                mine = mine + times(feats[c], state[c, p].astype(BF16))
                mixed = mixed + blend_ref[c + 1 : c + 2, lanes] * (
                    mine[:, :PAIR] / mine[:, PAIR:]
                )
                gone = rows_product(
                    fkw[c][:TILE], jnp.concatenate([values[:TILE], plain_ones], 1)
                )
                state[c, p] = state[c, p] + jnp.where(block, gone, 0.0)
            att_ref[here, lanes] = mixed.astype(BF16)
        return carry

    lax.fori_loop(0, rows // TILE, step, 0)
    for p in range(pairs):
        lanes = slice(p * PAIR, (p + 1) * PAIR)
        for c in range(2):
            last = rows_product(
                fk[c, rows:, lanes], jnp.concatenate([vpad[rows:, lanes], plain_ones], 1)
            )
            total_ref[c, p] = state[c, p] + jnp.where(block, last, 0.0)


def attend_back_kernel(
    rows, width, meta_ref, blend_ref, qkv_ref, halo_ref, state_ref, later_ref, go_ref,
    gqkv_ref, ghalo_ref, mix_ref, total_ref,
    kpad, vpad, fq, fk, state, gk, gv, gfk, gon,
):
    pairs = width // PAIR
    tiles = rows // TILE
    fill_features(meta_ref, qkv_ref, halo_ref, kpad, vpad, fq, fk, rows, width)
    state[...] = state_ref[...]
    mix_ref[...] = jnp.zeros_like(mix_ref)
    gk[...] = jnp.zeros_like(gk)
    gv[...] = jnp.zeros_like(gv)
    gfk[...] = jnp.zeros_like(gfk)
    ones = jnp.where(
        (lax.broadcasted_iota(jnp.int32, (2 * PAIR, PAIR), 0) // PAIR)
        == (lax.broadcasted_iota(jnp.int32, (2 * PAIR, PAIR), 1) // HEAD),
        1.0,
        0.0,
    ).astype(BF16)
    block = same_head(PAIR, 2 * PAIR)
    heads = jnp.where(same_head(2 * PAIR, PAIR), 1.0, 0.0).astype(BF16)
    plain_ones = jnp.ones((TILE, PAIR), BF16)
    high = (lax.broadcasted_iota(jnp.int32, (TILE, PAIR), 1) % HEAD) < HEAD // 2

    def step(tile, carry):
        at = pl.multiple_of(tile * TILE, TILE)
        here, window = pl.ds(at, TILE), pl.ds(at, 2 * TILE)
        near_mask, far_mask = tile_masks(meta_ref, tile)
        for p in range(pairs):
            lanes = slice(p * PAIR, (p + 1) * PAIR)
            q = qkv_ref[here, lanes]
            keys = split_heads(kpad[window, lanes])
            values = vpad[window, lanes]
            wide = jnp.concatenate([split_heads(values), ones], 1)
            feats = [fq[c, here, lanes] for c in range(2)]
            fkw = [fk[c, window, lanes] for c in range(2)]
            fks = [split_heads(f) for f in fkw]
            scores = tile_scores(q, keys, feats, fks, near_mask, far_mask)
            stack = jnp.concatenate(scores, 0).astype(BF16)
            sums = times(stack, wide)
            past = [state[c, p].astype(BF16) for c in range(2)]
            go = go_ref[here, lanes]
            outs = [sums[:TILE, :PAIR]]
            scales = [jnp.broadcast_to(blend_ref[0:1, lanes], (TILE, PAIR))]
            for c in range(2):
                mine = sums[(c + 1) * TILE : (c + 2) * TILE] + times(feats[c], past[c])
                inverse = 1.0 / mine[:, PAIR:]
                outs.append(mine[:, :PAIR] * inverse)
                scales.append(blend_ref[c + 1 : c + 2, lanes] * inverse)
            prods = [go * out for out in outs]
            for c in range(3):
                mix_ref[c : c + 1, lanes] += jnp.sum(prods[c], axis=0, keepdims=True)
            prod = jnp.concatenate(prods, 0)
            prod_low = prod.astype(BF16)
            rest = (prod - prod_low.astype(F32)).astype(BF16)
            deltas = times(jnp.concatenate([prod_low, rest], 1), heads)
            grads = []
            for c in range(3):
                delta = scales[c] * deltas[c * TILE : (c + 1) * TILE] * (-2.0 / HEAD)
                delta_low = delta.astype(BF16).astype(F32)
                delta = jnp.where(high, delta_low, delta - delta_low)
                grads.append(jnp.concatenate([scales[c] * go, delta], 1).astype(BF16))
            back = times_transposed(jnp.concatenate(grads, 0), wide)
            ds = (scores[0] * back[:TILE]).astype(BF16)
            gas = [
                jnp.where(far_mask, back[(c + 1) * TILE : (c + 2) * TILE], 0.0).astype(BF16)
                for c in range(2)
            ]
            q32 = q.astype(F32)
            small = jnp.exp(jnp.minimum(q32, 0.0))
            bent = jnp.tanh(q32)
            slopes = [jnp.where(q32 > 0, 1.0, small), 1.0 - bent * bent]
            gq = times(ds, keys)
            for c in range(2):
                gq = gq + slopes[c] * (
                    times(gas[c], fks[c]) + times_transposed(grads[c + 1], past[c])
                )
            gqkv_ref[here, lanes] = gq.astype(BF16)

            def tall(block):
                return jnp.concatenate([block[:, :PAIR], block[:, PAIR:]], 0)

            gk[window, lanes] += rows_product(tall(ds), split_heads(q * 0.125))
            for c in range(2):
                gfk[c, window, lanes] += rows_product(tall(gas[c]), split_heads(feats[c]))
            gv[window, lanes] += rows_product(
                jnp.concatenate([tall(stack[c * TILE : (c + 1) * TILE]) for c in range(3)], 0),
                jnp.concatenate([split_heads(g[:, :PAIR]) for g in grads], 0),
            )
            for c in range(2):
                gon[c, here, p * 2 * PAIR : (p + 1) * 2 * PAIR] = grads[c + 1]
                gone = rows_product(
                    fkw[c][:TILE], jnp.concatenate([values[:TILE], plain_ones], 1)
                )
                state[c, p] = state[c, p] + jnp.where(block, gone, 0.0)
        return carry

    lax.fori_loop(0, tiles, step, 0)
    ghalo_ref[:, :width] = gk[:TILE, :].astype(BF16)
    ghalo_ref[:, width:] = gv[:TILE, :].astype(BF16)
    state[...] = later_ref[...]
    length, offset = meta_ref[0], meta_ref[1]

    def add_later(at):
        here = pl.ds(at, TILE)
        for p in range(pairs):
            lanes = slice(p * PAIR, (p + 1) * PAIR)
            for c in range(2):
                come = rows_product(
                    fq[c, here, lanes], gon[c, here, p * 2 * PAIR : (p + 1) * 2 * PAIR]
                )
                state[c, p] = state[c, p] + jnp.where(block, come, 0.0)

    def back_step(step, carry):
        tile = tiles - 1 - step

        @pl.when(step >= 2)
        def _():
            add_later(pl.multiple_of((tile + 2) * TILE, TILE))

        at = pl.multiple_of(tile * TILE, TILE)
        here, there = pl.ds(at, TILE), pl.ds(at + TILE, TILE)
        position = offset + at + lax.broadcasted_iota(jnp.int32, (TILE, PAIR), 0)
        valid = position < length
        for p in range(pairs):
            lanes = slice(p * PAIR, (p + 1) * PAIR)
            values = vpad[there, lanes]
            wide = jnp.concatenate([values, plain_ones], 1)
            k32 = qkv_ref[here, width + p * PAIR : width + (p + 1) * PAIR].astype(F32)
            small = jnp.exp(jnp.minimum(k32, 0.0))
            bent = jnp.tanh(k32)
            slopes = [jnp.where(k32 > 0, 1.0, small), 1.0 - bent * bent]
            grad_k = gk[there, lanes]
            grad_v = gv[there, lanes]
            for c in range(2):
                later = state[c, p].astype(BF16)
                grad_f = gfk[c, there, lanes] + times_transposed(wide, later)
                grad_k = grad_k + jnp.where(valid, slopes[c] * grad_f, 0.0)
                grad_v = grad_v + times(fk[c, there, lanes], later[:, :PAIR])
            gqkv_ref[here, width + p * PAIR : width + (p + 1) * PAIR] = grad_k.astype(BF16)
            gqkv_ref[here, 2 * width + p * PAIR : 2 * width + (p + 1) * PAIR] = grad_v.astype(BF16)
        return carry

    lax.fori_loop(0, tiles, back_step, 0)
    add_later(TILE)
    add_later(0)
    total_ref[...] = state[...]


def attention_specs(rows, width):
    smem = pl.BlockSpec(memory_space=pltpu.SMEM)
    vmem = pl.BlockSpec(memory_space=pltpu.VMEM)
    scratch = [
        pltpu.VMEM((rows + TILE, width), BF16),
        pltpu.VMEM((rows + TILE, width), BF16),
        pltpu.VMEM((2, rows, width), BF16),
        pltpu.VMEM((2, rows + TILE, width), BF16),
        pltpu.VMEM((2, width // PAIR, PAIR, 2 * PAIR), F32),
    ]
    return smem, vmem, scratch


def attend(meta, blend, qkv, halo, state):
    rows, width = qkv.shape[0], qkv.shape[1] // 3
    smem, vmem, scratch = attention_specs(rows, width)
    return pl.pallas_call(
        functools.partial(attend_kernel, rows, width),
        out_shape=(
            jax.ShapeDtypeStruct((rows, width), BF16),
            jax.ShapeDtypeStruct(state.shape, F32),
        ),
        in_specs=[smem] + [vmem] * 4,
        out_specs=(vmem, vmem),
        scratch_shapes=scratch,
        compiler_params=pltpu.CompilerParams(vmem_limit_bytes=48 * 2**20),
        cost_estimate=pl.CostEstimate(
            flops=rows * width * 2 * 1024, bytes_accessed=rows * width * 8, transcendentals=0
        ),
    )(meta, blend, qkv, halo, state)


def attend_back(meta, blend, qkv, halo, state, later, go):
    rows, width = qkv.shape[0], qkv.shape[1] // 3
    smem, vmem, scratch = attention_specs(rows, width)
    return pl.pallas_call(
        functools.partial(attend_back_kernel, rows, width),
        out_shape=(
            jax.ShapeDtypeStruct((rows, 3 * width), BF16),
            jax.ShapeDtypeStruct((TILE, 2 * width), BF16),
            jax.ShapeDtypeStruct((3, width), F32),
            jax.ShapeDtypeStruct(state.shape, F32),
        ),
        in_specs=[smem] + [vmem] * 6,
        out_specs=(vmem,) * 4,
        scratch_shapes=scratch
        + [
            pltpu.VMEM((rows + TILE, width), F32),
            pltpu.VMEM((rows + TILE, width), F32),
            pltpu.VMEM((2, rows + TILE, width), F32),
            pltpu.VMEM((2, rows, 2 * width), BF16),
        ],
        compiler_params=pltpu.CompilerParams(vmem_limit_bytes=56 * 2**20),
        cost_estimate=pl.CostEstimate(
            flops=rows * width * 2 * 4096, bytes_accessed=rows * width * 16, transcendentals=0
        ),
    )(meta, blend, qkv, halo, state, later, go)


def to_sequences(block, axis, groups):
    return lax.all_to_all(block, axis, 0, 0, axis_index_groups=groups)


def from_parts(total, axis, parts, stride, forward):
    size = lax.axis_size(axis)
    low = total.astype(BF16)
    result = jnp.zeros_like(total)
    for hop in range(1, parts):
        distance = hop * stride
        route = [
            (i, i + distance) if forward else (i + distance, i) for i in range(size - distance)
        ]
        result = result + lax.ppermute(low, axis, route).astype(F32)
    return result


def local(
    inputs,
    cotangent,
    lengths,
    norm1_gain,
    norm1_bias,
    qkv_weight,
    blend_weights,
    out_weight,
    norm2_gain,
    norm2_bias,
    in_weight,
    in_bias,
    down_weight,
    down_bias,
):
    seqs, span, width = inputs.shape
    heads = blend_weights.shape[1]
    devices = lax.axis_size("seq")
    parts = devices // seqs
    rows = seqs * span
    index = lax.axis_index("seq")
    groups = None
    if parts > 1:
        groups = [[r * seqs + s for s in range(seqs)] for r in range(parts)]
    mine, part = index % seqs, index // seqs
    meta = jnp.stack([lax.dynamic_index_in_dim(lengths, mine, 0, False), part * rows])
    blend = jnp.repeat(blend_weights, width // heads, axis=1)

    x = to_sequences(inputs, "seq", groups).reshape(rows, width).astype(F32)
    grad_out = to_sequences(cotangent, "seq", groups).reshape(rows, width)

    normed, norm1_back = jax.vjp(layer_norm, x, norm1_gain, norm1_bias)
    normed_low = normed.astype(BF16)
    qkv = times(normed_low, qkv_weight).astype(BF16)
    halo = jnp.zeros((TILE, 2 * width), BF16)
    state = jnp.zeros((2, width // PAIR, PAIR, 2 * PAIR), F32)
    later = state
    if parts > 1:
        onward = [(i, i + seqs) for i in range(devices - seqs)]
        halo = lax.ppermute(qkv[rows - TILE :, width:], "seq", onward)
        total = attend(meta, blend, qkv, halo, state)[1]
        state = from_parts(total, "seq", parts, seqs, True)
    attended = attend(meta, blend, qkv, halo, state)[0]
    first = x + times(attended, out_weight)
    second, norm2_back = jax.vjp(layer_norm, first, norm2_gain, norm2_bias)
    second_low = second.astype(BF16)
    pre = times(second_low, in_weight) + in_bias
    hidden, gelu_back = jax.vjp(jax.nn.gelu, pre)
    hidden_low = hidden.astype(BF16)
    result = (first + times(hidden_low, down_weight) + down_bias).astype(BF16)
    output = to_sequences(result.reshape(seqs, span, width), "seq", groups)

    grad_out_f = grad_out.astype(F32)
    grad_down_w = rows_product(hidden_low, grad_out)
    grad_down_b = jnp.sum(grad_out_f, axis=0)
    (grad_pre,) = gelu_back(times_transposed(grad_out, down_weight))
    grad_pre_low = grad_pre.astype(BF16)
    grad_in_b = jnp.sum(grad_pre_low.astype(F32), axis=0)
    grad_in_w = rows_product(second_low, grad_pre_low)
    grad_first_part, grad_gain2, grad_bias2 = norm2_back(times_transposed(grad_pre_low, in_weight))
    grad_first = grad_out_f + grad_first_part
    grad_att_low = grad_first.astype(BF16)
    grad_out_w = rows_product(attended, grad_att_low)
    grad_o = times_transposed(grad_att_low, out_weight)

    if parts > 1:
        total = attend_back(meta, blend, qkv, halo, state, later, grad_o)[3]
        later = from_parts(total, "seq", parts, seqs, False)
    grad_qkv, grad_halo, mix, _ = attend_back(meta, blend, qkv, halo, state, later, grad_o)
    if parts > 1:
        homeward = [(i + seqs, i) for i in range(devices - seqs)]
        back = lax.ppermute(grad_halo, "seq", homeward)
        tail = grad_qkv[rows - TILE :, width:].astype(F32) + back.astype(F32)
        grad_qkv = grad_qkv.at[rows - TILE :, width:].set(tail.astype(BF16))
    grad_blend = jnp.sum(mix.reshape(3, heads, width // heads), axis=-1)
    grad_qkv_w = rows_product(normed_low, grad_qkv)
    grad_x_part, grad_gain1, grad_bias1 = norm1_back(times_transposed(grad_qkv, qkv_weight))
    grad_x = (grad_first + grad_x_part).astype(BF16)
    input_grad = to_sequences(grad_x.reshape(seqs, span, width), "seq", groups)
    summed = lax.psum(
        (
            grad_gain1,
            grad_bias1,
            grad_qkv_w,
            grad_blend,
            grad_out_w,
            grad_gain2,
            grad_bias2,
            grad_in_w,
            grad_in_b,
            grad_down_w,
            grad_down_b,
        ),
        ("seq", "batch"),
    )
    return (output, input_grad) + tuple(summed)


def solution(mesh):
    rows = P("batch", "seq", None)
    return jax.shard_map(
        local,
        mesh=mesh,
        in_specs=(rows, rows, P("batch")) + (P(),) * 11,
        out_specs=(rows, rows) + (P(),) * 11,
        check_vma=False,
    )
```

time: 994 us -> 500 us (0.50)
  waiting for transfers between devices: 390 us -> 219 us
  blocking collectives: 199 us -> 56 us
  other arithmetic: 146 us -> 11.3 us
  Pallas kernels: 0 us -> 105 us
  matrix products: 143 us -> 55 us
  local copies, waits for them, and re-layouts: 85.7 us -> 17.6 us
  starting transfers between devices: 7.73 us -> 21.3 us
    all_gather x4 -> x0, waiting for transfers between devices: 215 us -> none  [the longest x2 136 us: entering(): lax.all_gather(part.astype(kind), axis)]
    all_gather x4 -> x0, blocking collectives: 160 us -> none  [the longest x2 79.9 us: carried_in(): lax.all_gather(part.astype(kind), axis)]
    pallas_call x0 -> x2, Pallas kernels: none -> 105 us  [the longest x1 77.6 us: attend_back(): pl.pallas_call(functools.partial(attend_back_kernel, rows, width), out_sh...]
    select_n x32 -> x0, other arithmetic: 99.3 us -> none  [the longest x16 52.2 us: entering_hop(): return jax.tree.map(lambda a, b: jnp.where(reached, a, b), new, before)]
    dot_general x34 -> x4, matrix products: 113 us -> 17.6 us  [times(): lax.dot_general(left, right, (((1,), (0,)), ((), ())), preferred_element_...]
    all_to_all x0 -> x4, waiting for transfers between devices: none -> 52.9 us  [to_sequences(): return lax.all_to_all(block, axis, 0, 0, axis_index_groups=groups)]
    all_to_all x0 -> x4, starting transfers between devices: none -> 21.2 us  [to_sequences(): return lax.all_to_all(block, axis, 0, 0, axis_index_groups=groups)]
    unnamed x249 -> x76, local copies, waits for them, and re-layouts: 37.1 us -> 16.7 us
  transfers between devices with their start and end apart: 7 -> 5, of which waited for: 4 -> 3; matrix products, arithmetic and copies ran while one was open for 22% -> 6% of each run, Pallas kernels for 0% -> 5%
where the time goes in v1:
time: 500 us; the launch traced here: 499 us
  waiting for transfers between devices  219 us (44%)
  Pallas kernels  105 us (21%)
  blocking collectives  56 us (11%)
  matrix products  55 us (11%)
  starting transfers between devices  21.3 us (4%)
  local copies, waits for them, and re-layouts  17.6 us (4%)
  between operations  14.4 us (3%)
  other arithmetic  11.3 us (2%)
    psum x1, waiting for transfers between devices, local(): lax.psum((grad_gain1, grad_bias1, grad_qkv_w, grad_blend, grad_out_w, gra...  166 us
    pallas_call x1, Pallas kernels, attend_back(): pl.pallas_call(functools.partial(attend_back_kernel, rows, width), out_sh...  77.6 us
    psum x1, blocking collectives, local(): lax.psum((grad_gain1, grad_bias1, grad_qkv_w, grad_blend, grad_out_w, gra...  56 us
    all_to_all x4, waiting for transfers between devices, to_sequences(): return lax.all_to_all(block, axis, 0, 0, axis_index_groups=groups)  52.9 us
    pallas_call x1, Pallas kernels, attend(): pl.pallas_call(functools.partial(attend_kernel, rows, width), out_shape=(...  27.1 us
    all_to_all x4, starting transfers between devices, to_sequences(): return lax.all_to_all(block, axis, 0, 0, axis_index_groups=groups)  21.2 us
    dot_general x4, matrix products, times_transposed(): lax.dot_general(left, right, (((1,), (1,)), ((), ())), preferred_element_...  19.8 us
    dot_general x4, matrix products, times(): lax.dot_general(left, right, (((1,), (0,)), ((), ())), preferred_element_...  17.6 us
  transfers between devices with their start and end apart: 5, of which 3 were waited for; matrix products, arithmetic and copies ran while one was open for 6% of the time, Pallas kernels for 5%

profile of v1, /device:TPU:0, one launch (start us, length us, event | category | flops | bytes accessed | tf_op | source)
XLA Modules:
  0.0 498.9 jit_solution(732414084047811643)
XLA Ops:
  7.2 7.4 %all-to-all-start = ((bf16[8,128,512]{2,1,0:T(8,128)(2,1)}), bf16[8,128,512]{2,1,0:T(8,128)(2,1)S(1)}, u32[]{:S(2)}, u32[]{:S(2)}) async-start(bf16[8,128,512]{2,1,0:T(8,128)(2,1)} %param.14), calls=%async_computation | async-start | bytes 2097152 | tf_op jit(solution)/shard_map/all_to_all | solution.py:383
  16.1 24.3 %all-to-all-done = bf16[8,128,512]{2,1,0:T(8,128)(2,1)S(1)} async-done(((bf16[8,128,512]{2,1,0:T(8,128)(2,1)}), bf16[8,128,512]{2,1,0:T(8,128)(2,1)S(1)}, u32[]{:S(2)}, u32[]{:S(2)}) %all-to-all-start) | async-done | bytes 1048608 | tf_op jit(solution)/shard_map/all_to_all | solution.py:383
  40.4 4.3 all-to-all-start.2
  46.1 3.5 convolution_convert_fusion.qkv_ref
  49.8 27.1 %shard_map.237 = (bf16[1024,512]{1,0:T(8,128)(2,1)S(1)}, f32[2,4,128,256]{3,2,1,0:T(8,128)}) custom-call(s32[2]{0:T(128)S(1)} %pad_add_fusion.meta_ref, f32[3,512]{1,0:T(4,128)S(1)} %reshape.129.blend_ref, bf16[1024,1536]{1,0:T(8,128)(2,1)} %convolution_convert_fusion.qkv_ref, bf16[64,1024]{1,0:T(8,128)(2,1)S(1)} %broadcast_in_dim.15.halo_ref, ...), custom_call_target="tpu_custom_call" | custom-call | flops 1073741824 | bytes 4194304 | tf_op jit(solution)/shard_map/pallas_call | solution.py:339
  79.1 7.2 %multiply_convert_fusion = (bf16[1024,2048]{1,0:T(8,128)(2,1)}, f32[1024,2048]{1,0:T(8,128)}) fusion(f32[2048]{0:T(1024)S(1)} %copy-done.31, bf16[512,2048]{1,0:T(8,128)(2,1)S(1)} %copy-done, f32[1024,512]{1,0:T(8,128)S(1)} %get-tuple-element.42, f32[512]{0:T(512)S(1)} %copy-done.26, f32[512]{0:T(512)S(1)} %copy-done.24, f32[1024]{0:T(1024)S(1)} %fusion.22, ...), kind=kOutput, calls=%fused_computation.10 | convolution fusion | flops 2171076608 | bytes 16797696 | tf_op jit(solution)/shard_map/dot_general | solution.py:39
  86.3 10.4 %convert_reduce_fusion = (f32[2048]{0:T(1024)S(1)}, bf16[1024,2048]{1,0:T(8,128)(2,1)S(1)}) fusion(f32[1024,2048]{1,0:T(8,128)} %get-tuple-element.44, f32[2048]{0:T(1024)S(1)} %copy-done.31, bf16[1024,512]{1,0:T(8,128)(2,1)} %bitcast.5, bf16[2048,512]{1,0:T(8,128)(2,1)} %param.26), kind=kOutput, calls=%fused_computation.9 | convolution fusion | flops 2195716096 | bytes 15745024 | tf_op jit(solution)/shard_map/dot_general | solution.py:33
  96.8 2.9 multiply_reduce_fusion
  100.6 2.3 fusion.18
  102.9 2.0 fusion.30.go_ref
  104.9 1.7 fusion.32
  106.7 4.7 fusion.25
  111.4 77.6 %shard_map.238 = (bf16[1024,1536]{1,0:T(8,128)(2,1)}, bf16[64,1024]{1,0:T(8,128)(2,1)}, f32[3,512]{1,0:T(4,128)}, f32[2,4,128,256]{3,2,1,0:T(8,128)}) custom-call(s32[2]{0:T(128)} %copy-done.7, f32[3,512]{1,0:T(4,128)} %copy-done.6, bf16[1024,1536]{1,0:T(8,128)(2,1)} %convolution_convert_fusion.qkv_ref, bf16[64,1024]{1,0:T(8,128)(2,1)} %copy-done.5, ...), custom_call_target="tpu_custom_call" | custom-call | flops 4294967296 | bytes 8388608 | tf_op jit(solution)/shard_map/pallas_call | solution.py:358
  189.0 5.5 %fusion.31 = f32[512,1536]{1,0:T(8,128)} fusion(bf16[1024,512]{1,0:T(8,128)(2,1)S(1)} %copy-done.23, bf16[1024,1536]{1,0:T(8,128)(2,1)} %get-tuple-element.17), kind=kOutput, calls=%fused_computation.60 | convolution fusion | flops 1610612736 | bytes 7340032 | tf_op jit(solution)/shard_map/dot_general | solution.py:27
  194.5 5.6 %fusion.33 = f32[2048,512]{1,0:T(8,128)} fusion(bf16[1024,2048]{1,0:T(8,128)(2,1)S(1)} %copy-done.34, bf16[1024,512]{1,0:T(8,128)(2,1)} %bitcast.5), kind=kOutput, calls=%fused_computation.62 | convolution fusion | flops 2147483648 | bytes 9437184 | tf_op jit(solution)/shard_map/dot_general | solution.py:27
  200.2 1.6 copy-done.13
  201.7 6.2 %add_convert_fusion.1 = bf16[1024,512]{1,0:T(8,128)(2,1)} fusion(f32[1024,512]{1,0:T(8,128)S(1)} %copy-done.13, bf16[1024,2048]{1,0:T(8,128)(2,1)} %get-tuple-element.43, bf16[2048,512]{1,0:T(8,128)(2,1)} %param.26, f32[512]{0:T(512)S(1)} %copy-done.32), kind=kOutput, calls=%fused_computation.34 | convolution fusion | flops 2149056512 | bytes 9439232 | tf_op jit(solution)/shard_map/dot_general | solution.py:39
  207.9 6.0 %all-to-all-start.1 = ((bf16[8,128,512]{2,1,0:T(8,128)(2,1)}), bf16[8,128,512]{2,1,0:T(8,128)(2,1)S(1)}, u32[]{:S(2)}, u32[]{:S(2)}) async-start(bf16[8,128,512]{2,1,0:T(8,128)(2,1)} %bitcast.4), calls=%async_computation.1 | async-start | bytes 2097152 | tf_op jit(solution)/shard_map/all_to_all | solution.py:383
  213.9 4.5 fusion.27
  218.4 1.2 fusion.14
  220.0 3.0 add_convert_fusion
  222.9 28.6 %all-to-all-done.1 = bf16[8,128,512]{2,1,0:T(8,128)(2,1)S(1)} async-done(((bf16[8,128,512]{2,1,0:T(8,128)(2,1)}), bf16[8,128,512]{2,1,0:T(8,128)(2,1)S(1)}, u32[]{:S(2)}, u32[]{:S(2)}) %all-to-all-start.1) | async-done | bytes 1048608 | tf_op jit(solution)/shard_map/all_to_all | solution.py:383
  251.5 3.6 all-to-all-start.3
  255.3 1.5 convert_reduce_fusion.2
  256.7 56.0 %all-reduce = (f32[512]{0:T(512)}, f32[512]{0:T(512)}, f32[3,8]{1,0:T(4,128)}, f32[512]{0:T(512)}, f32[512]{0:T(512)}, /*index=5*/f32[2048]{0:T(1024)}, f32[512]{0:T(512)}) all-reduce(f32[512]{0:T(512)S(1)} %get-tuple-element.21, f32[512]{0:T(512)S(1)} %get-tuple-element.24, ...), channel_id=1, replica_groups=mesh['seq'=8,'batch'=4] {'seq','batch'}, use_global_device_ids=true, to_apply=%region_9.10 | all-reduce | flops 4632 | bytes 37056 | tf_op jit(solution)/shard_map/psum | solution.py:479
  312.7 165.9 %all-reduce.4.cloned.1.call-done = (f32[512,1536]{1,0:T(8,128)}, f32[512,512]{1,0:T(8,128)}, f32[512,2048]{1,0:T(8,128)}, f32[2048,512]{1,0:T(8,128)}) async-done(((f32[512,1536]{1,0:T(8,128)}, f32[512,512]{1,0:T(8,128)}, f32[512,2048]{1,0:T(8,128)}, f32[2048,512]{1,0:T(8,128)}), (f32[512,1536]{1,0:T(8,128)}, f32[512,512]{1,0:T(8,128)}, f32[512,2048]{1,0:T(8,128)}, ...) | async-done | bytes 12582928 | tf_op jit(solution)/shard_map/psum | solution.py:479
  478.6 1.0 copy.33
  481.2 1.7 copy.35
  484.1 1.1 copy-done.17
  485.2 2.1 copy.37
  487.4 1.6 copy-done.16
  488.9 2.1 copy.38
  (95 shorter events, 10.6 us)
Async XLA Ops:
  7.2 72.0 %copy-start = (bf16[512,2048]{1,0:T(8,128)(2,1)S(1)}, bf16[512,2048]{1,0:T(8,128)(2,1)}, u32[]{:S(2)}) copy-start(bf16[512,2048]{1,0:T(8,128)(2,1)} %param.24) | copy-start | bytes 6291460
  7.2 7.4 %copy-start.28 = (f32[3,8]{1,0:T(4,128)S(1)}, f32[3,8]{1,0:T(4,128)}, u32[]{:S(2)}) copy-start(f32[3,8]{1,0:T(4,128)} %param.20) | copy-start | bytes 292
  7.2 7.6 %copy-start.33 = (s32[8]{0:T(128)S(1)}, s32[8]{0:T(128)}, u32[]{:S(2)}) copy-start(s32[8]{0:T(128)} %param.16) | copy-start | bytes 100
  7.2 33.2 %all-to-all-start = ((bf16[8,128,512]{2,1,0:T(8,128)(2,1)}), bf16[8,128,512]{2,1,0:T(8,128)(2,1)S(1)}, u32[]{:S(2)}, u32[]{:S(2)}) async-start(bf16[8,128,512]{2,1,0:T(8,128)(2,1)} %param.14), calls=%async_computation | async-start | bytes 2097152 | tf_op jit(solution)/shard_map/all_to_all | solution.py:383
  14.8 34.9 %copy-start.6 = (f32[3,512]{1,0:T(4,128)}, f32[3,512]{1,0:T(4,128)S(1)}, u32[]{:S(2)}) copy-start(f32[3,512]{1,0:T(4,128)S(1)} %reshape.129.blend_ref) | copy-start | bytes 18436
  16.1 33.6 %copy-start.7 = (s32[2]{0:T(128)}, s32[2]{0:T(128)S(1)}, u32[]{:S(2)}) copy-start(s32[2]{0:T(128)S(1)} %pad_add_fusion.meta_ref) | copy-start | bytes 28
  16.1 29.4 %copy-start.25 = (f32[512]{0:T(512)S(1)}, f32[512]{0:T(512)}, u32[]{:S(2)}) copy-start(f32[512]{0:T(512)} %param.17) | copy-start | bytes 6148
  16.1 29.4 %copy-start.29 = (f32[512]{0:T(512)S(1)}, f32[512]{0:T(512)}, u32[]{:S(2)}) copy-start(f32[512]{0:T(512)} %param.18) | copy-start | bytes 6148
  40.4 5.1 %copy-start.8 = (bf16[8,128,512]{2,1,0:T(8,128)(2,1)}, bf16[8,128,512]{2,1,0:T(8,128)(2,1)S(1)}, u32[]{:S(2)}) copy-start(bf16[8,128,512]{2,1,0:T(8,128)(2,1)S(1)} %all-to-all-done) | copy-start | bytes 3145732
  40.4 45.9 %all-to-all-start.2 = ((bf16[8,128,512]{2,1,0:T(8,128)(2,1)}), bf16[8,128,512]{2,1,0:T(8,128)(2,1)}, u32[]{:S(2)}, u32[]{:S(2)}) async-start(bf16[8,128,512]{2,1,0:T(8,128)(2,1)} %param.15), calls=%async_computation.2 | async-start | bytes 2097152 | tf_op jit(solution)/shard_map/all_to_all | solution.py:383
  44.7 433.9 %all-reduce.4.cloned.1.call-start = ((), (), s32[]{:S(2)}) async-start(), calls=%async_computation.4 | async-start | bytes 25165824 | tf_op jit(solution)/shard_map/psum | solution.py:479
  46.1 3.5 copy-start.22
  49.6 27.2 %copy-start.5 = (bf16[64,1024]{1,0:T(8,128)(2,1)}, bf16[64,1024]{1,0:T(8,128)(2,1)S(1)}, u32[]{:S(2)}) copy-start(bf16[64,1024]{1,0:T(8,128)(2,1)S(1)} %broadcast_in_dim.15.halo_ref) | copy-start | bytes 393220
  49.7 27.1 %copy-start.2 = (f32[2,4,128,256]{3,2,1,0:T(8,128)}, f32[2,4,128,256]{3,2,1,0:T(8,128)S(1)}, u32[]{:S(2)}) copy-start(f32[2,4,128,256]{3,2,1,0:T(8,128)S(1)} %broadcast_in_dim.16.state_ref.later_ref) | copy-start | bytes 3145732
  49.7 27.1 %copy-start.9 = (bf16[8,128,512]{2,1,0:T(8,128)(2,1)S(1)}, bf16[8,128,512]{2,1,0:T(8,128)(2,1)}, u32[]{:S(2)}) copy-start(bf16[8,128,512]{2,1,0:T(8,128)(2,1)} %copy-done.8) | copy-start | bytes 3145732
  49.8 27.1 %copy-start.19 = (bf16[512,512]{1,0:T(8,128)(2,1)S(1)}, bf16[512,512]{1,0:T(8,128)(2,1)}, u32[]{:S(2)}) copy-start(bf16[512,512]{1,0:T(8,128)(2,1)} %param.21) | copy-start | bytes 1572868
  86.3 10.4 %copy-start.12 = (f32[1024,512]{1,0:T(8,128)S(1)}, f32[1024,512]{1,0:T(8,128)}, u32[]{:S(2)}) copy-start(f32[1024,512]{1,0:T(8,128)} %copy-done.11) | copy-start | bytes 6291460
  100.5 2.3 copy-start.14
  100.6 2.3 copy-start.20
  102.9 2.1 copy-start.4
  111.4 77.6 %copy-start.23 = (bf16[1024,512]{1,0:T(8,128)(2,1)S(1)}, bf16[1024,512]{1,0:T(8,128)(2,1)}, u32[]{:S(2)}) copy-start(bf16[1024,512]{1,0:T(8,128)(2,1)} %copy-done.22) | copy-start | bytes 3145732
  189.0 5.5 %copy-start.34 = (bf16[1024,2048]{1,0:T(8,128)(2,1)S(1)}, bf16[1024,2048]{1,0:T(8,128)(2,1)}, u32[]{:S(2)}) copy-start(bf16[1024,2048]{1,0:T(8,128)(2,1)} %get-tuple-element.43) | copy-start | bytes 12582916
  207.9 6.0 %copy-start.10 = (bf16[8,128,512]{2,1,0:T(8,128)(2,1)S(1)}, bf16[8,128,512]{2,1,0:T(8,128)(2,1)}, u32[]{:S(2)}) copy-start(bf16[8,128,512]{2,1,0:T(8,128)(2,1)} %copy-done.8) | copy-start | bytes 3145732
  207.9 43.6 %all-to-all-start.1 = ((bf16[8,128,512]{2,1,0:T(8,128)(2,1)}), bf16[8,128,512]{2,1,0:T(8,128)(2,1)S(1)}, u32[]{:S(2)}, u32[]{:S(2)}) async-start(bf16[8,128,512]{2,1,0:T(8,128)(2,1)} %bitcast.4), calls=%async_computation.1 | async-start | bytes 2097152 | tf_op jit(solution)/shard_map/all_to_all | solution.py:383
  218.4 1.6 copy-start.15
  222.9 32.1 %copy-start.27 = (f32[3,512]{1,0:T(4,128)S(1)}, f32[3,512]{1,0:T(4,128)}, u32[]{:S(2)}) copy-start(f32[3,512]{1,0:T(4,128)} %get-tuple-element.18) | copy-start | bytes 18436
  251.5 61.2 %all-to-all-start.3 = ((bf16[8,128,512]{2,1,0:T(8,128)(2,1)}), bf16[8,128,512]{2,1,0:T(8,128)(2,1)S(1)}, u32[]{:S(2)}, u32[]{:S(2)}) async-start(bf16[8,128,512]{2,1,0:T(8,128)(2,1)} %bitcast.6), calls=%async_computation.3 | async-start | bytes 2097152 | tf_op jit(solution)/shard_map/all_to_all | solution.py:383
  478.5 2.6 copy-start.18
  481.2 2.0 copy-start.21
  481.2 4.0 copy-start.17
  485.2 3.7 copy-start.16
  488.9 3.1 copy-start.1
  (8 other events, 10.8 us)
Sparse Core Ops, SparseCore 0:
  200.3 278.2 all-reduce.3
